TPU v7x, 512 devices: a whole 4x8x8 slice. The times are simulated.
512 devices in a mesh: section: 4 (over y_hi), chan: 16 (over z, core), dp: 8 (over y_lo, x).
Axes of the slice: x: 4, y: 8 (y_hi: 4, y_lo: 2; y = y_hi * 2 + y_lo), z: 8, core: 2. Of those that a mesh axis runs over, the one named last changes fastest.
Arguments:
- images: bfloat16 [2560, 2048], P(('section', 'dp')), may hold values from -6 to 6
- conv_one: bfloat16 [3, 3, 2560, 5120], P(None, None, ('section', 'dp'), 'chan'), may hold values from -0.0390625 to 0.0390625
- conv_two: bfloat16 [3, 3, 5120, 5120], P(None, None, ('section', 'dp'), 'chan'), may hold values from -0.02734375 to 0.02734375
- mix_weight: bfloat16 [5120, 5120], P(('section', 'dp'), 'chan'), may hold values from -0.078125 to 0.078125
Outputs:
- block_out: bfloat16 [8, 64, 5120], P('dp', 'section', 'chan')
All inputs are finite; a program needn't handle non-finite values.
Results may differ from a plain program's by a relative error of at most 0.02.
Values may be sent and summed in bfloat16 or wider, within the bound.
A program may use at most 64 MiB of HBM per device.

v0:
```python
import jax
import jax.numpy as jnp
from jax import lax
from jax.sharding import PartitionSpec as P

HW = 16


def to_blocks(values, n_data, n_section):
    count, places, width = values.shape
    shaped = values.reshape(n_data, count // n_data, n_section, places // n_section, width)
    return shaped.transpose(2, 0, 1, 3, 4).reshape(-1, width)


def from_blocks(values, n_data, n_section, count, half):
    width = values.shape[1]
    places = half * half
    shaped = values.reshape(n_section, n_data, count // n_data, places // n_section, width)
    return shaped.transpose(1, 2, 0, 3, 4).reshape(count, half, half, width)


def per_device(images, conv_one, conv_two, mix_weight):
    n_section = lax.axis_size("section")
    n_data = lax.axis_size("dp")
    side = HW
    count = images.shape[1] // (side * side)
    half = side // 2
    rows = count * half * half
    in_local = images.shape[0]
    maps = images.reshape(in_local, count, side, side)
    padded = jnp.pad(maps, ((0, 0), (0, 0), (1, 1), (1, 1)))
    total = jnp.zeros((rows, conv_one.shape[3]), jnp.float32)
    for tap_a in range(3):
        for tap_b in range(3):
            window = padded[:, :, tap_a : tap_a + side : 2, tap_b : tap_b + side : 2].reshape(
                in_local, rows
            )
            total = total + lax.dot_general(
                window,
                conv_one[tap_a, tap_b],
                (((0,), (0,)), ((), ())),
                preferred_element_type=jnp.float32,
            )
    section_terms = to_blocks(total.reshape(count, half * half, -1), n_data, n_section)
    share_rows = rows // (n_section * n_data)
    summed = lax.psum(section_terms.astype(jnp.bfloat16), ("section", "dp"))
    skip = lax.dynamic_slice_in_dim(
        summed, lax.axis_index(("section", "dp")) * share_rows, share_rows, 0
    )
    rect_blocks = jnp.maximum(summed, 0)
    rectified = from_blocks(rect_blocks, n_data, n_section, count, half)
    padded_two = jnp.pad(rectified, ((0, 0), (1, 1), (1, 1), (0, 0)))
    inner = jnp.zeros((rows, conv_two.shape[2]), jnp.float32)
    for tap_a in range(3):
        for tap_b in range(3):
            window = padded_two[:, tap_a : tap_a + half, tap_b : tap_b + half, :].reshape(rows, -1)
            inner = inner + lax.dot_general(
                window,
                conv_two[tap_a, tap_b],
                (((1,), (1,)), ((), ())),
                preferred_element_type=jnp.float32,
            )
    inner_blocks = to_blocks(inner.reshape(count, half * half, -1), n_data, n_section)
    inner_sum = lax.psum(inner_blocks.astype(jnp.bfloat16), "chan").astype(jnp.float32)
    gated = jnp.maximum(inner_sum, 0.0).astype(jnp.bfloat16)
    mixed = lax.psum_scatter(
        jnp.dot(gated, mix_weight, preferred_element_type=jnp.float32).astype(jnp.bfloat16),
        ("section", "dp"),
        scatter_dimension=0,
        tiled=True,
    ).astype(jnp.float32)
    result = (mixed + skip.astype(jnp.float32)).astype(jnp.bfloat16)
    per_data = count // n_data
    return result.reshape(per_data, share_rows // per_data, -1)


def solution(mesh):
    in_specs = (
        P(("section", "dp"), None),
        P(None, None, ("section", "dp"), "chan"),
        P(None, None, ("section", "dp"), "chan"),
        P(("section", "dp"), "chan"),
    )
    out_specs = P("dp", "section", "chan")
    return jax.shard_map(
        per_device, mesh=mesh, in_specs=in_specs, out_specs=out_specs, check_vma=False
    )
```

profile of v0, /device:TPU:16, one launch (start us, length us, event | category | flops | bytes accessed | tf_op | source)
XLA Modules:
  0.0 522.6 jit_solution(15222768242337160034)
XLA Ops:
  6.5 1.3 copy.6
  8.1 1.5 slice.106
  9.6 1.5 slice.108
  11.0 1.6 slice.110
  12.6 1.5 slice.112
  14.1 1.5 slice.114
  15.6 1.6 slice.116
  17.2 1.5 slice.118
  18.6 1.5 slice.120
  20.1 1.6 slice.122
  21.7 0.3 fusion.30
  22.0 0.3 convolution_add_fusion.7
  22.3 0.3 convolution_add_fusion.6
  22.6 0.3 convolution_add_fusion.5
  22.9 0.3 convolution_add_fusion.4
  23.2 0.3 convolution_add_fusion.3
  23.5 0.3 convolution_add_fusion.2
  23.8 0.3 convolution_add_fusion.1
  24.1 0.3 fusion
  24.6 0.8 copy.8
  25.5 160.4 %all-reduce.5.cloned.1.call-done = bf16[512,320]{1,0:T(8,128)(2,1)} async-done(((bf16[512,320]{1,0:T(8,128)(2,1)}), bf16[512,320]{1,0:T(8,128)(2,1)}) %all-reduce.5.cloned.1.call-update) | async-done | bytes 327696 | tf_op jit(solution)/shard_map/psum | solution.py:46
  185.9 1.0 broadcast_maximum_fusion
  187.0 0.5 pad_slice_fusion
  187.5 0.7 copy-done.1
  189.1 0.3 convolution_add_fusion.13
  189.9 0.3 convolution_add_fusion.10
  190.5 0.3 fusion.1
  191.0 0.7 copy.11
  191.8 112.8 %all-reduce.7.cloned.1.call-done = bf16[512,160]{1,0:T(8,128)(2,1)} async-done(((bf16[512,160]{1,0:T(8,128)(2,1)}), bf16[512,160]{1,0:T(8,128)(2,1)}) %all-reduce.7.cloned.1.call-update) | async-done | bytes 163856 | tf_op jit(solution)/shard_map/psum | solution.py:64
  304.6 2.0 convolution_convert_fusion
  306.6 208.1 %reduce-scatter.2.cloned.1.call-done = bf16[16,320]{1,0:T(8,128)(2,1)} async-done(((bf16[512,320]{1,0:T(8,128)(2,1)}), bf16[16,320]{1,0:T(8,128)(2,1)}) %reduce-scatter.2.cloned.1.call-update) | async-done | bytes 10256 | tf_op jit(solution)/shard_map/reduce_scatter | solution.py:66
  514.8 1.3 fusion.41
  (21 shorter events, 2.5 us)
Async XLA Ops:
  6.5 298.1 %copy-start = (bf16[160,320]{1,0:T(8,128)(2,1)S(1)}, bf16[160,320]{1,0:T(8,128)(2,1)}, u32[]{:S(2)}) copy-start(bf16[160,320]{1,0:T(8,128)(2,1)} %param.7) | copy-start | bytes 307204
  6.5 179.4 %all-reduce.5.cloned.1.call-start = ((), (), s32[]{:S(2)}) async-start(), calls=%async_computation.1 | async-start | bytes 786432 | tf_op jit(solution)/shard_map/psum | solution.py:46
  9.5 12.2 %copy-start.2 = (bf16[3,3,80,320]{3,2,1,0:T(8,128)(2,1)S(1)}, bf16[3,3,80,320]{3,2,1,0:T(8,128)(2,1)}, u32[]{:S(2)}) copy-start(bf16[3,3,80,320]{3,2,1,0:T(8,128)(2,1)} %param.5) | copy-start | bytes 1382404
  25.4 279.2 %all-reduce.7.cloned.1.call-start = ((), (), s32[]{:S(2)}) async-start(), calls=%async_computation.2 | async-start | bytes 524288 | tf_op jit(solution)/shard_map/psum | solution.py:64
  187.0 1.2 copy-start.1
  191.7 323.0 %reduce-scatter.2.cloned.1.call-start = ((), (), s32[]{:S(2)}) async-start(), calls=%async_computation.3 | async-start | bytes 405504 | tf_op jit(solution)/shard_map/reduce_scatter | solution.py:66
Sparse Core Ops, SparseCore 0:
  25.6 160.2 all-reduce.4
  191.8 112.7 all-reduce.6
  309.0 205.6 reduce-scatter.1
where the time goes:
time: 523 us
  waiting for transfers between devices  481 us (92%)
  local copies, waits for them, and re-layouts  18.3 us (3%)
  between operations  13.4 us (3%)
  matrix products  7.12 us (1%)
    reduce_scatter x1, waiting for transfers between devices, per_device(): lax.psum_scatter(jnp.dot(gated, mix_weight, preferred_element_type=jnp.fl...  208 us
    psum x1, waiting for transfers between devices, per_device(): summed = lax.psum(section_terms.astype(jnp.bfloat16), ('section', 'dp'))  160 us
    psum x1, waiting for transfers between devices, per_device(): lax.psum(inner_blocks.astype(jnp.bfloat16), 'chan').astype(jnp.float32)  113 us
    slice x9, local copies, waits for them, and re-layouts, per_device(): padded[:, :, tap_a:tap_a + side:2, tap_b:tap_b + side:2]  13.6 us
  transfers between devices with their start and end apart: 3, of which 3 were waited for; matrix products, arithmetic and copies ran while one was open for 0% of the time, Pallas kernels for 0%

commit v1 on v0

--- a/solution.py
+++ b/solution.py
@@ -61,7 +61,9 @@
                 preferred_element_type=jnp.float32,
             )
     inner_blocks = to_blocks(inner.reshape(count, half * half, -1), n_data, n_section)
-    inner_sum = lax.psum(inner_blocks.astype(jnp.bfloat16), "chan").astype(jnp.float32)
+    inner_sum = jnp.sum(lax.all_gather(inner_blocks.astype(jnp.bfloat16), "chan"), axis=0).astype(
+        jnp.float32
+    )
     gated = jnp.maximum(inner_sum, 0.0).astype(jnp.bfloat16)
     mixed = lax.psum_scatter(
         jnp.dot(gated, mix_weight, preferred_element_type=jnp.float32).astype(jnp.bfloat16),

time: 523 us -> 451 us (0.86)
  waiting for transfers between devices: 481 us -> 408 us
    psum x1 -> x0, waiting for transfers between devices: 113 us -> none  [per_device(): lax.psum(inner_blocks.astype(jnp.bfloat16), 'chan').astype(jnp.float32)]
    all_gather x0 -> x1, waiting for transfers between devices: none -> 42 us  [per_device(): lax.all_gather(inner_blocks.astype(jnp.bfloat16), 'chan')]
where the time goes in v1:
time: 451 us
  waiting for transfers between devices  408 us (90%)
  local copies, waits for them, and re-layouts  18.3 us (4%)
  between operations  13.4 us (3%)
  matrix products  6.22 us (1%)
    reduce_scatter x1, waiting for transfers between devices, per_device(): lax.psum_scatter(jnp.dot(gated, mix_weight, preferred_element_type=jnp.fl...  206 us
    psum x1, waiting for transfers between devices, per_device(): summed = lax.psum(section_terms.astype(jnp.bfloat16), ('section', 'dp'))  160 us
    all_gather x1, waiting for transfers between devices, per_device(): lax.all_gather(inner_blocks.astype(jnp.bfloat16), 'chan')  42 us
    slice x9, local copies, waits for them, and re-layouts, per_device(): padded[:, :, tap_a:tap_a + side:2, tap_b:tap_b + side:2]  13.6 us
  transfers between devices with their start and end apart: 3, of which 3 were waited for; matrix products, arithmetic and copies ran while one was open for 0% of the time, Pallas kernels for 0%

profile of v1, /device:TPU:16, one launch (start us, length us, event | category | flops | bytes accessed | tf_op | source)
XLA Modules:
  0.0 450.9 jit_solution(2462024076281997590)
XLA Ops:
  6.5 1.3 copy.19
  8.1 1.5 slice.106
  9.6 1.5 slice.108
  11.0 1.6 slice.110
  12.6 1.5 slice.112
  14.1 1.5 slice.114
  15.6 1.6 slice.116
  17.2 1.5 slice.118
  18.6 1.5 slice.120
  20.1 1.6 slice.122
  21.7 0.3 fusion.30
  22.0 0.3 convolution_add_fusion.7
  22.3 0.3 convolution_add_fusion.6
  22.6 0.3 convolution_add_fusion.5
  22.9 0.3 convolution_add_fusion.4
  23.2 0.3 convolution_add_fusion.3
  23.5 0.3 convolution_add_fusion.2
  23.8 0.3 convolution_add_fusion.1
  24.1 0.3 fusion
  24.6 0.8 copy.21
  25.5 160.4 %all-reduce.4.cloned.1.call-done = bf16[512,320]{1,0:T(8,128)(2,1)} async-done(((bf16[512,320]{1,0:T(8,128)(2,1)}), bf16[512,320]{1,0:T(8,128)(2,1)}) %all-reduce.4.cloned.1.call-update) | async-done | bytes 327696 | tf_op jit(solution)/shard_map/psum | solution.py:46
  185.9 1.0 broadcast_maximum_fusion
  187.0 0.5 pad_slice_fusion
  187.5 0.7 copy-done.1
  189.9 0.3 convolution_add_fusion.10
  190.5 0.3 fusion.1
  191.0 0.8 copy.25
  191.8 42.0 %all-gather.2.cloned.1.call-done = bf16[16,512,160]{1,2,0:T(8,128)(2,1)} async-done(((bf16[1,512,160]{1,2,0:T(8,128)(2,1)}), bf16[16,512,160]{1,2,0:T(8,128)(2,1)}) %all-gather.2.cloned.1.call-update) | async-done | bytes 2621456 | tf_op jit(solution)/shard_map/all_gather | solution.py:64
  233.9 2.1 reduce_sum.12
  236.0 1.1 convolution_convert_fusion
  237.1 206.0 %reduce-scatter.2.cloned.1.call-done = bf16[16,320]{1,0:T(8,128)(2,1)} async-done(((bf16[512,320]{1,0:T(8,128)(2,1)}), bf16[16,320]{1,0:T(8,128)(2,1)}) %reduce-scatter.2.cloned.1.call-update) | async-done | bytes 10256 | tf_op jit(solution)/shard_map/reduce_scatter | solution.py:68
  443.1 1.3 fusion.41
  (23 shorter events, 2.8 us)
Async XLA Ops:
  6.5 229.4 %copy-start = (bf16[160,320]{1,0:T(8,128)(2,1)S(1)}, bf16[160,320]{1,0:T(8,128)(2,1)}, u32[]{:S(2)}) copy-start(bf16[160,320]{1,0:T(8,128)(2,1)} %param.7) | copy-start | bytes 307204
  6.5 179.3 %all-reduce.4.cloned.1.call-start = ((), (), s32[]{:S(2)}) async-start(), calls=%async_computation.1 | async-start | bytes 786432 | tf_op jit(solution)/shard_map/psum | solution.py:46
  9.5 12.2 %copy-start.2 = (bf16[3,3,80,320]{3,2,1,0:T(8,128)(2,1)S(1)}, bf16[3,3,80,320]{3,2,1,0:T(8,128)(2,1)}, u32[]{:S(2)}) copy-start(bf16[3,3,80,320]{3,2,1,0:T(8,128)(2,1)} %param.5) | copy-start | bytes 1382404
  25.4 208.4 %all-gather.2.cloned.1.call-start = ((), (), s32[]{:S(2)}) async-start(), calls=%async_computation.2 | async-start | bytes 2785280 | tf_op jit(solution)/shard_map/all_gather | solution.py:64
  187.0 1.2 copy-start.1
  191.8 251.3 %reduce-scatter.2.cloned.1.call-start = ((), (), s32[]{:S(2)}) async-start(), calls=%async_computation.3 | async-start | bytes 405504 | tf_op jit(solution)/shard_map/reduce_scatter | solution.py:68
Sparse Core Ops, SparseCore 0:
  25.6 160.2 all-reduce.3
  191.9 41.8 all-gather.1
  238.9 204.1 reduce-scatter.1
